TPU v7x, 256 devices: a whole 4x4x8 slice. The times are simulated.
256 devices in a mesh: ctx: 32 (over y, z), tp: 8 (over x, core).
Axes of the slice: x: 4, y: 4, z: 8, core: 2. Of those that a mesh axis runs over, the one named last changes fastest.
Arguments:
- queries: bfloat16 [16384, 8192], P('ctx', 'tp'), may hold values from -6 to 6
- keys: bfloat16 [16384, 8192], P('ctx', 'tp'), may hold values from -6 to 6
- values: bfloat16 [16384, 8192], P('ctx', 'tp'), may hold values from -75 to 75
- gate: bfloat16 [16384, 8192], P('ctx', 'tp'), may hold values from -6 to 6
- gain: float32 [8192], P('tp'), may hold values from 0.1 to 1.9
- out_grad: bfloat16 [16384, 8192], P('ctx', 'tp'), may hold values from -6 to 6
Outputs:
- output: bfloat16 [16384, 8192], P('ctx', 'tp')
- query_grad: bfloat16 [16384, 8192], P('ctx', 'tp')
- key_grad: bfloat16 [16384, 8192], P('ctx', 'tp')
- value_grad: bfloat16 [16384, 8192], P('ctx', 'tp')
- gate_grad: bfloat16 [16384, 8192], P('ctx', 'tp')
All inputs are finite; a program needn't handle non-finite values.
Results may differ from a plain program's by a relative error of at most 0.005.
Values sent between devices are 32-bit elements; how exact they have to be, the bound alone decides.
No kernel may reach another device: no remote copies, remote signals or barrier semaphores. Data moves between devices by JAX's collectives and lax.ppermute only.
A program may use at most 128 MiB of HBM per device.

v0:
```python
import jax
import jax.numpy as jnp
from jax import lax
from jax.sharding import PartitionSpec as P

HD = 128
BLOCK = 512
D = 8192
EPS = 1e-06


def carried_in(value, axis, join, neutral, backward):
    count, mine = (lax.axis_size(axis), lax.axis_index(axis))
    pieces = lax.all_gather(value, axis)
    if backward:
        pieces = pieces[::-1]
        mine = count - 1 - mine
    running = jnp.full_like(value, 0) + jnp.asarray(neutral, value.dtype)

    def turn(position, running):
        longer = join(running, pieces[position])
        return jnp.where(position < mine, longer, running)

    return lax.fori_loop(0, count - 1, turn, running)


def add_states(earlier, later):
    return earlier + later


def local(queries, keys, values, gate, gain, out_grad):
    tok_rows, width = queries.shape
    heads_here = width // HD
    nblocks = tok_rows // BLOCK
    high = lax.Precision.HIGHEST

    def split(x):
        return x.reshape(nblocks, BLOCK, heads_here, HD)

    q_blocks, k_blocks, v_blocks = (split(queries), split(keys), split(values))
    row_ids = lax.broadcasted_iota(jnp.int32, (BLOCK, BLOCK), 0)
    col_ids = lax.broadcasted_iota(jnp.int32, (BLOCK, BLOCK), 1)
    causal = col_ids <= row_ids
    scores = jnp.einsum("nbhe,nche->nhbc", q_blocks, k_blocks, preferred_element_type=jnp.float32)
    attn = jnp.where(causal, scores, 0.0).astype(jnp.bfloat16)
    block_kv = jnp.einsum("nche,nchf->nhef", k_blocks, v_blocks, preferred_element_type=jnp.float32)
    device_kv = jnp.sum(block_kv, 0)
    local_before = jnp.cumsum(block_kv, 0) - block_kv
    empty = jnp.zeros_like(device_kv)
    carried = carried_in(device_kv, "ctx", add_states, empty, False)
    states = carried[None] + local_before
    inter = jnp.einsum("nbhe,nhef->nbhf", q_blocks.astype(jnp.float32), states, precision=high)
    intra = jnp.einsum("nhbc,nchf->nbhf", attn, v_blocks, preferred_element_type=jnp.float32)
    mixed = (intra + inter).reshape(tok_rows, width)
    sig = jax.nn.sigmoid(gate.astype(jnp.float32))
    dy_full = out_grad.astype(jnp.float32)
    dn = dy_full * gain * sig
    own_square = jnp.sum(mixed * mixed, axis=1)
    square_total = lax.psum(own_square, "tp")
    inv_rms = lax.rsqrt(square_total / D + EPS)[:, None]
    normed = mixed * inv_rms
    output = (normed * gain * sig).astype(jnp.bfloat16)
    cross_total = lax.psum(jnp.sum(dn * mixed, axis=1), "tp")
    project = inv_rms * (cross_total / D)[:, None]
    mixed_grad = (inv_rms * (dn - normed * project)).astype(jnp.bfloat16)
    gate_grad = (dy_full * gain * normed * sig * (1.0 - sig)).astype(jnp.bfloat16)
    d_blocks = split(mixed_grad)
    prob = jnp.where(
        causal,
        jnp.einsum("nbhf,nchf->nhbc", d_blocks, v_blocks, preferred_element_type=jnp.float32),
        0.0,
    ).astype(jnp.bfloat16)
    q_grad = jnp.einsum("nhbc,nche->nbhe", prob, k_blocks, preferred_element_type=jnp.float32)
    q_grad = q_grad + jnp.einsum(
        "nbhf,nhef->nbhe", d_blocks.astype(jnp.float32), states, precision=high
    )
    block_g = jnp.einsum("nbhe,nbhf->nhef", q_blocks, d_blocks, preferred_element_type=jnp.float32)
    local_after = jnp.flip(jnp.cumsum(jnp.flip(block_g, 0), 0), 0) - block_g
    device_g = jnp.sum(block_g, 0)
    later = carried_in(device_g, "ctx", add_states, empty, True)
    after = later[None] + local_after
    k_grad = jnp.einsum("nhbc,nbhe->nche", prob, q_blocks, preferred_element_type=jnp.float32)
    k_grad = k_grad + jnp.einsum(
        "nchf,nhef->nche", v_blocks.astype(jnp.float32), after, precision=high
    )
    v_grad = jnp.einsum("nhbc,nbhf->nchf", attn, d_blocks, preferred_element_type=jnp.float32)
    v_grad = v_grad + jnp.einsum(
        "nche,nhef->nchf", k_blocks.astype(jnp.float32), after, precision=high
    )
    return (
        output,
        q_grad.reshape(tok_rows, width).astype(jnp.bfloat16),
        k_grad.reshape(tok_rows, width).astype(jnp.bfloat16),
        v_grad.reshape(tok_rows, width).astype(jnp.bfloat16),
        gate_grad,
    )


def solution(mesh):
    return jax.shard_map(
        local,
        mesh=mesh,
        in_specs=(
            P("ctx", "tp"),
            P("ctx", "tp"),
            P("ctx", "tp"),
            P("ctx", "tp"),
            P("tp"),
            P("ctx", "tp"),
        ),
        out_specs=(P("ctx", "tp"), P("ctx", "tp"), P("ctx", "tp"), P("ctx", "tp"), P("ctx", "tp")),
        check_vma=False,
    )
```

profile of v0, /device:TPU:1, one launch (start us, length us, event | category | flops | bytes accessed | tf_op | source)
XLA Modules:
  0.0 434.1 jit_solution(13185674936705253317)
XLA Ops:
  7.2 2.6 copy.67
  9.8 1.6 copy.39
  11.4 2.9 fusion.9
  14.5 2.6 select_convert_fusion.1
  17.1 2.1 copy-done.1
  19.2 2.8 fusion.4
  22.0 136.4 %all-gather.5.cloned.1.call-done = f32[256,128,128]{2,1,0:T(8,128)} async-done(((f32[8,128,128]{2,1,0:T(8,128)}), f32[256,128,128]{2,1,0:T(8,128)}) %all-gather.5.cloned.1.call-update) | async-done | bytes 16777232 | tf_op jit(solution)/shard_map/all_gather | solution.py:14
  158.5 38.8 %while.28 = (s32[]{:T(128)}, f32[8,128,128]{2,1,0:T(8,128)S(1)}, s32[]{:T(128)}, f32[32,8,128,128]{3,2,1,0:T(8,128)}, s32[]{:T(128)}, /*index=5*/s32[]{:T(128)}) while((s32[]{:T(128)}, f32[8,128,128]{2,1,0:T(8,128)S(1)}, s32[]{:T(128)}, f32[32,8,128,128]{3,2,1,0:T(8,128)}, s32[]{:T(128)}, /*index=5*/s32[]{:T(128)}) %tuple.79), condition=%wide.region_1.2_spmd.clone, body=%wide.region_0.1_spmd.clone.sunk | while | flops 393220 | bytes 1572965 | solution.py:24
  158.5 1.3 add_select_fusion.4
  159.8 1.2 add_select_fusion.4
  161.0 1.2 add_select_fusion.4
  162.3 1.2 add_select_fusion.4
  163.5 1.2 add_select_fusion.4
  164.8 1.2 add_select_fusion.4
  166.0 1.2 add_select_fusion.4
  167.3 1.2 add_select_fusion.4
  168.5 1.2 add_select_fusion.4
  169.8 1.2 add_select_fusion.4
  171.0 1.2 add_select_fusion.4
  172.3 1.2 add_select_fusion.4
  173.5 1.2 add_select_fusion.4
  174.8 1.2 add_select_fusion.4
  176.0 1.2 add_select_fusion.4
  177.3 1.2 add_select_fusion.4
  178.5 1.2 add_select_fusion.4
  179.8 1.2 add_select_fusion.4
  189.8 1.2 add_select_fusion.4
  197.3 4.1 fusion.2
  201.4 3.0 copy.43
  204.4 2.6 multiply_reduce_fusion
  207.0 13.0 %all-reduce = (f32[512]{0:T(512)S(1)}, f32[512]{0:T(512)S(1)}) all-reduce(f32[512]{0:T(512)S(1)} %get-tuple-element.228, f32[512]{0:T(512)S(1)} %multiply_reduce_fusion), channel_id=1, replica_groups=mesh['ctx'=32,'tp'=8] {'tp'}, use_global_device_ids=true, to_apply=%region_3.4 | all-reduce | flops 1024 | bytes 8192 | tf_op jit(solution)/shard_map/psum | solution.py:59
  220.0 4.9 %multiply_convert_fusion = (bf16[512,1024]{1,0:T(8,128)(2,1)}, bf16[512,1024]{1,0:T(8,128)(2,1)}, bf16[512,1024]{1,0:T(8,128)(2,1)}) fusion(bf16[512,1024]{1,0:T(8,128)(2,1)S(1)} %copy-done.14, f32[512,1024]{1,0:T(8,128)} %copy.43, f32[1024]{0:T(1024)S(1)} %copy-done.15, f32[512]{0:T(512)S(1)} %get-tuple-element.227, bf16[512,1024]{1,0:T(8,128)(2,1)} %param.13, ...), kind=kLoop, calls=%fused_computation.11 | loop fusion | flops 10485760 | bytes 7348224 | tf_op jit(solution)/shard_map/convert_element_type | solution.py:66
  224.8 1.5 copy.63
  227.9 2.7 select_convert_fusion
  230.6 1.5 fusion.27
  232.6 2.1 fusion.1
  234.7 2.3 copy.58
  236.9 4.5 %fusion.28 = f32[8,128,512]{2,1,0:T(8,128)} fusion(bf16[512,8,128]{0,2,1:T(8,128)(2,1)S(1)} %bitcast.119, bf16[8,512,512]{2,1,0:T(8,128)(2,1)} %copy-done.1), kind=kOutput, calls=%fused_computation.49 | convolution fusion | flops 536870912 | bytes 7340032 | tf_op jit(solution)/shard_map/nhbc,nbhf->nchf/dot_general | solution.py:86
  241.4 123.1 %all-gather.7.cloned.1.call-done = f32[256,128,128]{2,1,0:T(8,128)} async-done(((f32[8,128,128]{2,1,0:T(8,128)}), f32[256,128,128]{2,1,0:T(8,128)}) %all-gather.7.cloned.1.call-update) | async-done | bytes 16777232 | tf_op jit(solution)/shard_map/all_gather | solution.py:14
  364.5 11.7 %rev.3 = f32[32,8,128,128]{3,2,1,0:T(8,128)} reverse(f32[32,8,128,128]{3,2,1,0:T(8,128)} %bitcast.120), dimensions={0} | reverse | bytes 33554432 | tf_op jit(solution)/shard_map/rev | solution.py:16
  376.2 38.9 %while.29 = (s32[]{:T(128)}, f32[8,128,128]{2,1,0:T(8,128)S(1)}, s32[]{:T(128)}, f32[32,8,128,128]{3,2,1,0:T(8,128)}, s32[]{:T(128)}, /*index=5*/s32[]{:T(128)}) while((s32[]{:T(128)}, f32[8,128,128]{2,1,0:T(8,128)S(1)}, s32[]{:T(128)}, f32[32,8,128,128]{3,2,1,0:T(8,128)}, s32[]{:T(128)}, /*index=5*/s32[]{:T(128)}) %tuple.72), condition=%wide.region_7.8_spmd.clone, body=%wide.region_6.7_spmd.clone.sunk | while | flops 393220 | bytes 1572965 | solution.py:24
  376.2 1.3 add_select_fusion.5
  391.4 1.2 add_select_fusion.5
  392.6 1.2 add_select_fusion.5
  416.2 3.6 fusion.6
  420.9 1.3 copy.60
  422.3 3.7 fusion
  425.9 1.3 copy.59
  (83 shorter events, 53.4 us)
Async XLA Ops:
  7.2 7.3 %copy-start = (bf16[512,1024]{1,0:T(8,128)(2,1)S(1)}, bf16[512,1024]{1,0:T(8,128)(2,1)}, u32[]{:S(2)}) copy-start(bf16[512,1024]{1,0:T(8,128)(2,1)} %param.10) | copy-start | bytes 3145732
  7.2 151.3 %all-gather.5.cloned.1.call-start = ((), (), s32[]{:S(2)}) async-start(), calls=%async_computation | async-start | bytes 17301504 | tf_op jit(solution)/shard_map/all_gather | solution.py:14
  11.4 5.7 %copy-start.3 = (bf16[512,8,128]{0,2,1:T(8,128)(2,1)}, bf16[512,8,128]{0,2,1:T(8,128)(2,1)S(1)}, u32[]{:S(2)}) copy-start(bf16[512,8,128]{0,2,1:T(8,128)(2,1)S(1)} %copy.39) | copy-start | bytes 3145732
  14.3 350.2 %all-gather.7.cloned.1.call-start = ((), (), s32[]{:S(2)}) async-start(), calls=%async_computation.1 | async-start | bytes 17301504 | tf_op jit(solution)/shard_map/all_gather | solution.py:14
  14.5 4.7 %copy-start.5 = (bf16[512,1024]{1,0:T(8,128)(2,1)S(1)}, bf16[512,1024]{1,0:T(8,128)(2,1)}, u32[]{:S(2)}) copy-start(bf16[512,1024]{1,0:T(8,128)(2,1)} %param.12) | copy-start | bytes 3145732
  17.1 2.1 copy-start.1
  158.5 38.8 %copy-start.7 = (f32[8,128,128]{2,1,0:T(8,128)S(1)}, f32[8,128,128]{2,1,0:T(8,128)}, u32[]{:S(2)}) copy-start(f32[8,128,128]{2,1,0:T(8,128)} %fusion.9) | copy-start | bytes 1572868
  201.4 3.0 copy-start.14
  201.4 3.0 copy-start.15
  226.8 1.0 copy-start.10
  227.8 2.7 copy-start.4
  230.6 2.0 copy-start.2
  230.6 2.0 copy-start.8
  376.2 39.9 %copy-start.6 = (bf16[512,1024]{1,0:T(8,128)(2,1)S(1)}, bf16[512,1024]{1,0:T(8,128)(2,1)}, u32[]{:S(2)}) copy-start(bf16[512,1024]{1,0:T(8,128)(2,1)} %param.12) | copy-start | bytes 3145732
  376.2 39.9 %copy-start.11 = (f32[8,128,128]{1,2,0:T(8,128)S(1)}, f32[8,128,128]{1,2,0:T(8,128)}, u32[]{:S(2)}) copy-start(f32[8,128,128]{1,2,0:T(8,128)} %copy-done.10) | copy-start | bytes 1572868
  416.1 3.6 copy-start.9
  416.1 3.6 copy-start.12
  416.2 3.6 copy-start.13
Sparse Core Ops, SparseCore 0:
  14.4 143.9 all-gather.4
  228.0 136.5 all-gather.6
where the time goes:
time: 437 us; the launch traced here: 434 us
  waiting for transfers between devices  260 us (59%)
  other arithmetic  83.8 us (19%)
  matrix products  32 us (7%)
  local copies, waits for them, and re-layouts  29.9 us (7%)
  between operations  14.3 us (3%)
  blocking collectives  13 us (3%)
    all_gather x2, waiting for transfers between devices, carried_in(): pieces = lax.all_gather(value, axis)  260 us
    select_n x62, other arithmetic, turn(): return jnp.where(position < mine, longer, running)  76.2 us
    psum x1, blocking collectives, local(): square_total = lax.psum(own_square, 'tp')  13 us
    rev x1, local copies, waits for them, and re-layouts, carried_in(): pieces = pieces[::-1]  11.7 us
    unnamed x36, local copies, waits for them, and re-layouts  10.1 us
  transfers between devices with their start and end apart: 2, of which 2 were waited for; matrix products, arithmetic and copies ran while one was open for 4% of the time, Pallas kernels for 0%

commit v1 on v0

--- a/solution.py
+++ b/solution.py
@@ -56,7 +56,7 @@
     dy_full = out_grad.astype(jnp.float32)
     dn = dy_full * gain * sig
     own_square = jnp.sum(mixed * mixed, axis=1)
-    square_total = lax.psum(own_square, "tp")
+    square_total = jnp.sum(lax.all_gather(own_square, "tp"), axis=0)
     inv_rms = lax.rsqrt(square_total / D + EPS)[:, None]
     normed = mixed * inv_rms
     output = (normed * gain * sig).astype(jnp.bfloat16)

time: 437 us -> 452 us (1.034)
  blocking collectives: 13 us -> 26.4 us
    all_gather x0 -> x1, blocking collectives: none -> 13.6 us  [local(): square_total = jnp.sum(lax.all_gather(own_square, 'tp'), axis=0)]
    unnamed x36 -> x38, local copies, waits for them, and re-layouts: 10.1 us -> 12.2 us
where the time goes in v1:
time: 452 us; the launch traced here: 449 us
  waiting for transfers between devices  259 us (57%)
  other arithmetic  83.8 us (19%)
  local copies, waits for them, and re-layouts  32 us (7%)
  matrix products  31.6 us (7%)
  blocking collectives  26.4 us (6%)
  between operations  14.3 us (3%)
    all_gather x2, waiting for transfers between devices, carried_in(): pieces = lax.all_gather(value, axis)  259 us
    select_n x62, other arithmetic, turn(): return jnp.where(position < mine, longer, running)  76.2 us
    all_gather x1, blocking collectives, local(): square_total = jnp.sum(lax.all_gather(own_square, 'tp'), axis=0)  13.6 us
    psum x1, blocking collectives, local(): cross_total = lax.psum(jnp.sum(dn * mixed, axis=1), 'tp')  12.8 us
    unnamed x38, local copies, waits for them, and re-layouts  12.2 us
    rev x1, local copies, waits for them, and re-layouts, carried_in(): pieces = pieces[::-1]  11.7 us
  transfers between devices with their start and end apart: 2, of which 2 were waited for; matrix products, arithmetic and copies ran while one was open for 4% of the time, Pallas kernels for 0%

profile of v1, /device:TPU:1, one launch (start us, length us, event | category | flops | bytes accessed | tf_op | source)
XLA Modules:
  0.0 449.0 jit_solution(16661713911482261704)
XLA Ops:
  7.2 2.6 copy.67
  9.8 1.6 copy.39
  11.5 1.3 fusion.9
  13.0 2.5 select_convert_fusion.1
  15.5 2.1 copy-done.1
  17.6 2.9 fusion.4
  20.4 136.5 %all-gather.7.cloned.1.call-done = f32[256,128,128]{2,1,0:T(8,128)} async-done(((f32[8,128,128]{2,1,0:T(8,128)}), f32[256,128,128]{2,1,0:T(8,128)}) %all-gather.7.cloned.1.call-update) | async-done | bytes 16777232 | tf_op jit(solution)/shard_map/all_gather | solution.py:14
  156.9 38.8 %while.28 = (s32[]{:T(128)}, f32[8,128,128]{2,1,0:T(8,128)S(1)}, s32[]{:T(128)}, f32[32,8,128,128]{3,2,1,0:T(8,128)}, s32[]{:T(128)}, /*index=5*/s32[]{:T(128)}) while((s32[]{:T(128)}, f32[8,128,128]{2,1,0:T(8,128)S(1)}, s32[]{:T(128)}, f32[32,8,128,128]{3,2,1,0:T(8,128)}, s32[]{:T(128)}, /*index=5*/s32[]{:T(128)}) %tuple.79), condition=%wide.region_1.2_spmd.clone, body=%wide.region_0.1_spmd.clone.sunk | while | flops 393220 | bytes 1572965 | solution.py:24
  156.9 1.3 add_select_fusion.4
  158.2 1.2 add_select_fusion.4
  159.5 1.2 add_select_fusion.4
  160.7 1.2 add_select_fusion.4
  162.0 1.2 add_select_fusion.4
  163.2 1.2 add_select_fusion.4
  164.5 1.2 add_select_fusion.4
  165.8 1.2 add_select_fusion.4
  167.0 1.2 add_select_fusion.4
  168.3 1.2 add_select_fusion.4
  169.5 1.2 add_select_fusion.4
  170.8 1.2 add_select_fusion.4
  172.0 1.2 add_select_fusion.4
  173.3 1.2 add_select_fusion.4
  174.5 1.2 add_select_fusion.4
  175.8 1.2 add_select_fusion.4
  182.0 1.2 add_select_fusion.4
  195.8 4.1 fusion.2
  199.8 3.0 copy.43
  202.9 2.6 multiply_reduce_fusion
  205.5 12.8 %psum.7 = f32[512]{0:T(512)S(1)} all-reduce(f32[512]{0:T(512)S(1)} %multiply_reduce_fusion), channel_id=1, replica_groups=mesh['ctx'=32,'tp'=8] {'tp'}, use_global_device_ids=true, to_apply=%region_5.6 | all-reduce | flops 512 | bytes 4096 | tf_op jit(solution)/shard_map/psum | solution.py:63
  218.3 13.6 %all-gather.3 = f32[8,1,512]{2,1,0:T(1,128)S(1)} all-gather(f32[1,1,512]{2,1,0:T(1,128)S(1)} %bitcast.129), channel_id=3, replica_groups=mesh['ctx'=32,'tp'=8] {'tp'}, dimensions={0}, use_global_device_ids=true | all-gather | bytes 18432 | tf_op jit(solution)/shard_map/all_gather | solution.py:59
  231.9 4.9 %multiply_convert_fusion = (bf16[512,1024]{1,0:T(8,128)(2,1)}, bf16[512,1024]{1,0:T(8,128)(2,1)}, bf16[512,1024]{1,0:T(8,128)(2,1)}) fusion(bf16[512,1024]{1,0:T(8,128)(2,1)S(1)} %copy-done.15, f32[512,1024]{1,0:T(8,128)} %copy.43, f32[1024]{0:T(1024)S(1)} %copy-done.16, f32[512]{0:T(512)S(1)} %get-tuple-element.225, bf16[512,1024]{1,0:T(8,128)(2,1)} %param.13, ...), kind=kLoop, calls=%fused_computation.11 | loop fusion | flops 10485760 | bytes 7348224 | tf_op jit(solution)/shard_map/convert_element_type | solution.py:66
  236.8 1.5 copy.63
  239.8 2.7 select_convert_fusion
  242.6 1.5 fusion.27
  244.5 2.1 fusion.1
  246.6 2.3 copy.58
  248.9 4.4 fusion.28
  253.3 122.8 %all-gather.9.cloned.1.call-done = f32[256,128,128]{2,1,0:T(8,128)} async-done(((f32[8,128,128]{2,1,0:T(8,128)}), f32[256,128,128]{2,1,0:T(8,128)}) %all-gather.9.cloned.1.call-update) | async-done | bytes 16777232 | tf_op jit(solution)/shard_map/all_gather | solution.py:14
  376.1 11.7 %rev.3 = f32[32,8,128,128]{3,2,1,0:T(8,128)} reverse(f32[32,8,128,128]{3,2,1,0:T(8,128)} %bitcast.121), dimensions={0} | reverse | bytes 33554432 | tf_op jit(solution)/shard_map/rev | solution.py:16
  387.8 38.9 %while.29 = (s32[]{:T(128)}, f32[8,128,128]{2,1,0:T(8,128)S(1)}, s32[]{:T(128)}, f32[32,8,128,128]{3,2,1,0:T(8,128)}, s32[]{:T(128)}, /*index=5*/s32[]{:T(128)}) while((s32[]{:T(128)}, f32[8,128,128]{2,1,0:T(8,128)S(1)}, s32[]{:T(128)}, f32[32,8,128,128]{3,2,1,0:T(8,128)}, s32[]{:T(128)}, /*index=5*/s32[]{:T(128)}) %tuple.72), condition=%wide.region_7.8_spmd.clone, body=%wide.region_6.7_spmd.clone.sunk | while | flops 393220 | bytes 1572965 | solution.py:24
  387.8 1.3 add_select_fusion.5
  406.7 1.2 add_select_fusion.5
  408.0 1.2 add_select_fusion.5
  427.8 3.6 fusion.6
  431.4 2.1 add_convert_fusion
  433.5 2.4 copy.60
  435.9 4.0 fusion
  439.9 2.3 copy.59
  (87 shorter events, 54.8 us)
Async XLA Ops:
  7.2 5.8 %copy-start = (bf16[512,1024]{1,0:T(8,128)(2,1)S(1)}, bf16[512,1024]{1,0:T(8,128)(2,1)}, u32[]{:S(2)}) copy-start(bf16[512,1024]{1,0:T(8,128)(2,1)} %param.10) | copy-start | bytes 3145732
  7.2 149.8 %all-gather.7.cloned.1.call-start = ((), (), s32[]{:S(2)}) async-start(), calls=%async_computation | async-start | bytes 17301504 | tf_op jit(solution)/shard_map/all_gather | solution.py:14
  7.2 4.3 copy-start.5
  11.5 1.3 copy-start.3
  12.8 363.3 %all-gather.9.cloned.1.call-start = ((), (), s32[]{:S(2)}) async-start(), calls=%async_computation.1 | async-start | bytes 17301504 | tf_op jit(solution)/shard_map/all_gather | solution.py:14
  15.5 2.1 copy-start.1
  156.9 38.8 %copy-start.7 = (f32[8,128,128]{2,1,0:T(8,128)S(1)}, f32[8,128,128]{2,1,0:T(8,128)}, u32[]{:S(2)}) copy-start(f32[8,128,128]{2,1,0:T(8,128)} %fusion.9) | copy-start | bytes 1572868
  199.8 3.0 copy-start.15
  199.8 3.0 copy-start.16
  238.7 1.0 copy-start.10
  239.8 2.7 copy-start.4
  242.5 2.0 copy-start.2
  242.5 2.0 copy-start.8
  387.8 39.9 %copy-start.6 = (bf16[512,1024]{1,0:T(8,128)(2,1)S(1)}, bf16[512,1024]{1,0:T(8,128)(2,1)}, u32[]{:S(2)}) copy-start(bf16[512,1024]{1,0:T(8,128)(2,1)} %param.12) | copy-start | bytes 3145732
  387.8 39.9 %copy-start.11 = (f32[8,128,128]{1,2,0:T(8,128)S(1)}, f32[8,128,128]{1,2,0:T(8,128)}, u32[]{:S(2)}) copy-start(f32[8,128,128]{1,2,0:T(8,128)} %copy-done.10) | copy-start | bytes 1572868
  427.7 3.6 copy-start.9
  427.8 3.6 copy-start.13
  427.8 3.6 copy-start.14
  433.5 2.4 copy-start.12
Sparse Core Ops, SparseCore 0:
  12.9 143.9 all-gather.6
  239.9 136.1 all-gather.8
